TPU v7x, 256 devices: a whole 4x4x8 slice. The times are simulated.
256 devices in a mesh: seq: 128 (over y_hi, x, z, core), head: 2 (over y_lo).
Axes of the slice: x: 4, y: 4 (y_hi: 2, y_lo: 2; y = y_hi * 2 + y_lo), z: 8, core: 2. Of those that a mesh axis runs over, the one named last changes fastest.
Arguments:
- queries: bfloat16 [16384, 2560], P('seq', 'head'), may hold values from -6 to 6
- keys: bfloat16 [16384, 2560], P('seq', 'head'), may hold values from -6 to 6
- values: bfloat16 [16384, 2560], P('seq', 'head'), may hold values from -6 to 6
- grad_out: bfloat16 [16384, 2560], P('seq', 'head'), may hold values from -6 to 6
- cache: bfloat16 [16384, 2560], P('seq', 'head'), may hold values from -6 to 6
- w_kv: bfloat16 [2, 2560, 2560], P(None, 'seq', 'head'), may hold values from -0.125 to 0.125
- doc_ids: int32 [16384], replicated, may hold values from 0 to 127, never falling along the last dimension, each value on 1 to 256 neighbouring positions
- routes: int32 [16384], replicated, may hold values from 0 to 127, as said below
Outputs:
- output: bfloat16 [16384, 2560], P('seq', 'head')
- grad_q: bfloat16 [16384, 2560], P('seq', 'head')
- grad_k: bfloat16 [16384, 2560], P('seq', 'head')
- grad_v: bfloat16 [16384, 2560], P('seq', 'head')
Inputs may be any that keep to these rules, and one draw needn't show every extreme that they name: `routes`: each device's aligned block of 128 rows names every destination at most 2 times; in every draw some destination is named exactly 2 times by every block.
All inputs are finite; a program needn't handle non-finite values.
Results may differ from a plain program's by a relative error of at most 0.03.
Values may be sent and summed in bfloat16 or wider, within the bound.
A program may use at most 128 MiB of HBM per device.

v0:
```python
import jax
import jax.numpy as jnp
from jax import lax
from jax.sharding import PartitionSpec as P

HD = 128
SPAN = 2


def shifted(value, axis, by):
    length = lax.axis_size(axis)
    pairs = [(i, i + by) for i in range(length) if 0 <= i + by < length]
    return lax.ppermute(value, axis, pairs)


def attend(queries, key_set, value_set, grad_out, allowed, head_count):
    seg_rows = queries.shape[0]
    key_len = key_set.shape[0]
    head_dim = queries.shape[1] // head_count
    scaling = head_dim ** (-0.5)
    q_heads = queries.reshape(seg_rows, head_count, head_dim)
    k_heads = key_set.reshape(key_len, head_count, head_dim)
    v_heads = value_set.reshape(key_len, head_count, head_dim)
    g_heads = grad_out.reshape(seg_rows, head_count, head_dim)
    scores = (
        jnp.einsum("qhd,khd->hqk", q_heads, k_heads, preferred_element_type=jnp.float32) * scaling
    )
    scores = jnp.where(allowed[None], scores, -1e30)
    row_max = jnp.max(scores, axis=-1, keepdims=True)
    weights = jnp.where(allowed[None], jnp.exp(scores - row_max), 0.0)
    prob = weights / jnp.sum(weights, axis=-1, keepdims=True)
    prob_b = prob.astype(jnp.bfloat16)
    output_b = jnp.einsum(
        "hqk,khd->qhd", prob_b, v_heads, preferred_element_type=jnp.float32
    ).astype(jnp.bfloat16)
    dprob = jnp.einsum("qhd,khd->hqk", g_heads, v_heads, preferred_element_type=jnp.float32)
    delta = jnp.sum(g_heads.astype(jnp.float32) * output_b.astype(jnp.float32), axis=-1)
    dscore_b = (prob * (dprob - jnp.transpose(delta)[:, :, None]) * scaling).astype(jnp.bfloat16)
    grad_q = jnp.einsum(
        "hqk,khd->qhd", dscore_b, k_heads, preferred_element_type=jnp.float32
    ).astype(jnp.bfloat16)
    grad_k = jnp.einsum("hqk,qhd->khd", dscore_b, q_heads, preferred_element_type=jnp.float32)
    grad_v = jnp.einsum("hqk,qhd->khd", prob_b, g_heads, preferred_element_type=jnp.float32)
    return (
        output_b.reshape(seg_rows, -1),
        grad_q.reshape(seg_rows, -1),
        grad_k.reshape(key_len, -1),
        grad_v.reshape(key_len, -1),
    )


def body(queries, keys, values, grad_out, cache, w_kv, doc_ids, routes):
    devices = lax.axis_size("seq")
    my_index = lax.axis_index("seq")
    seg_rows = queries.shape[0]
    features = queries.shape[1]
    head_count = features // HD
    cache_rows = cache.shape[0]
    capacity = 2 * cache_rows // devices
    slot_count = capacity * devices
    pad_rows = SPAN * seg_rows
    window = pad_rows + seg_rows
    full_cache = lax.all_gather(cache, "head", axis=1, tiled=True)
    own_routes = lax.dynamic_slice_in_dim(routes, my_index * cache_rows, cache_rows)
    targets = jnp.arange(devices, dtype=jnp.int32)
    onehot = (own_routes[:, None] == targets[None, :]).astype(jnp.float32)
    row_ids = jnp.arange(cache_rows, dtype=jnp.int32)
    earlier = (row_ids[None, :] < row_ids[:, None]).astype(jnp.float32)
    before = jnp.dot(earlier, onehot, preferred_element_type=jnp.float32)
    ranks = jnp.sum(before * onehot, axis=1).astype(jnp.int32)
    place = own_routes * capacity + ranks
    incoming = jnp.sum((routes.reshape(devices, cache_rows) == my_index).astype(jnp.int32), axis=1)
    live = (jnp.arange(capacity, dtype=jnp.int32)[None, :] < incoming[:, None]).reshape(slot_count)
    outgoing = jnp.zeros((slot_count, full_cache.shape[1]), jnp.bfloat16).at[place].set(full_cache)
    arrived = lax.all_to_all(
        outgoing.reshape(devices, capacity, full_cache.shape[1]),
        "seq",
        split_axis=0,
        concat_axis=0,
        tiled=True,
    )
    source_rows = arrived.reshape(slot_count, full_cache.shape[1])
    piece = lax.all_gather(w_kv, "seq", axis=1, tiled=True)
    proj_k = jnp.dot(source_rows, piece[0], preferred_element_type=jnp.float32)
    proj_v = jnp.dot(source_rows, piece[1], preferred_element_type=jnp.float32)
    mem_keys = proj_k.astype(jnp.bfloat16)
    mem_values = proj_v.astype(jnp.bfloat16)
    current = jnp.stack([keys, values], 0)
    received = [current]
    for cycle_step in range(SPAN):
        current = shifted(current, "seq", 1)
        received.append(current)
    window_kv = jnp.concatenate(received[::-1], axis=1)
    start = my_index * seg_rows
    id_pad = jnp.concatenate([jnp.full((pad_rows,), -1, jnp.int32), doc_ids])
    q_ids = lax.dynamic_slice_in_dim(doc_ids, start, seg_rows)
    k_ids = lax.dynamic_slice_in_dim(id_pad, start, window)
    q_pos = start + jnp.arange(seg_rows, dtype=jnp.int32)
    k_pos = start - pad_rows + jnp.arange(window, dtype=jnp.int32)
    allowed_win = (k_pos[None, :] <= q_pos[:, None]) & (k_ids[None, :] == q_ids[:, None])
    allowed = jnp.concatenate(
        [jnp.broadcast_to(live[None, :], (seg_rows, slot_count)), allowed_win], 1
    )
    key_set = jnp.concatenate([mem_keys, window_kv[0]], 0)
    value_set = jnp.concatenate([mem_values, window_kv[1]], 0)
    output, grad_q, grad_k, grad_v = attend(
        queries, key_set, value_set, grad_out, allowed, head_count
    )
    pairs = jnp.stack([grad_k[slot_count:], grad_v[slot_count:]], 0)

    def piece_for(offset):
        lower = (SPAN - offset) * seg_rows
        return pairs[:, lower : lower + seg_rows]

    totals = piece_for(SPAN)
    for offset in range(SPAN - 1, -1, -1):
        totals = shifted(totals.astype(jnp.bfloat16), "seq", -1).astype(totals.dtype) + piece_for(
            offset
        )
    return (output, grad_q, totals[0].astype(jnp.bfloat16), totals[1].astype(jnp.bfloat16))


def solution(mesh):
    placed = (
        P("seq", "head"),
        P("seq", "head"),
        P("seq", "head"),
        P("seq", "head"),
        P("seq", "head"),
        P(None, "seq", "head"),
        P(),
        P(),
    )
    return jax.shard_map(
        body,
        mesh=mesh,
        in_specs=placed,
        out_specs=(P("seq", "head"), P("seq", "head"), P("seq", "head"), P("seq", "head")),
        check_vma=False,
    )
```

profile of v0, /device:TPU:231, one launch (start us, length us, event | category | flops | bytes accessed | tf_op | source)
XLA Modules:
  0.0 257.7 jit_solution(7245344041730218224)
XLA Ops:
  7.2 0.7 all-gather.2.cloned.1.call-update
  7.9 0.8 dynamic_slice.9
  8.8 9.5 %all_gather.6 = bf16[128,2560]{1,0:T(8,128)(2,1)S(1)} all-gather(bf16[128,1280]{1,0:T(8,128)(2,1)} %param.12), channel_id=1, replica_groups=mesh['seq'=128,'head'=2] {'head'}, dimensions={1}, use_global_device_ids=true | all-gather | bytes 983040 | tf_op jit(solution)/shard_map/all_gather | solution.py:63
  18.3 0.8 compare_select_fusion
  19.1 2.0 scatter_custom_fusion
  21.0 1.4 reshape.77
  22.4 13.8 %all-to-all-start = ((bf16[128,2,2560]{2,1,0:T(2,128)(2,1)}), bf16[128,2,2560]{2,1,0:T(2,128)(2,1)S(1)}, u32[]{:S(2)}, u32[]{:S(2)}) async-start(bf16[128,2,2560]{2,1,0:T(2,128)(2,1)} %reshape.77), calls=%async_computation | async-start | bytes 2621440 | tf_op jit(solution)/shard_map/all_to_all | solution.py:75
  36.3 0.2 copy.74
  36.5 0.2 copy.75
  36.8 4.9 %collective-permute-start = (bf16[2,128,1280]{1,2,0:T(8,128)(2,1)S(1)}, bf16[2,128,1280]{1,2,0:T(8,128)(2,1)}, u32[]{:S(2)}, u32[]{:S(2)}) collective-permute-start(bf16[2,128,1280]{1,2,0:T(8,128)(2,1)S(1)} %pad_maximum_fusion.7), channel_id=1, source_target_pairs={{0,2},{2,4},{4,6},{6,8},{8,10},{10,12},{12,14},{14,16},{16,18},{18... | collective-permute-start | bytes 1966088 | tf_op jit(solution)/shard_map/ppermute | solution.py:13
  42.3 1.2 copy.83
  43.5 30.5 %collective-permute-done = bf16[2,128,1280]{1,2,0:T(8,128)(2,1)} collective-permute-done((bf16[2,128,1280]{1,2,0:T(8,128)(2,1)S(1)}, bf16[2,128,1280]{1,2,0:T(8,128)(2,1)}, u32[]{:S(2)}, u32[]{:S(2)}) %collective-permute-start) | collective-permute-done | bytes 655392 | tf_op jit(solution)/shard_map/ppermute | solution.py:13
  74.1 10.3 %collective-permute-start.1 = (bf16[2,128,1280]{1,2,0:T(8,128)(2,1)}, bf16[2,128,1280]{1,2,0:T(8,128)(2,1)S(1)}, u32[]{:S(2)}, u32[]{:S(2)}) collective-permute-start(bf16[2,128,1280]{1,2,0:T(8,128)(2,1)} %collective-permute-done), channel_id=1, source_target_pairs={{0,2},{2,4},{4,6},{6,8},{8,10},{10,12},{12,14},{14,16},{16,18},{18... | collective-permute-start | bytes 1966088 | tf_op jit(solution)/shard_map/ppermute | solution.py:13
  84.8 8.2 %collective-permute-done.1 = bf16[2,128,1280]{1,2,0:T(8,128)(2,1)S(1)} collective-permute-done((bf16[2,128,1280]{1,2,0:T(8,128)(2,1)}, bf16[2,128,1280]{1,2,0:T(8,128)(2,1)S(1)}, u32[]{:S(2)}, u32[]{:S(2)}) %collective-permute-start.1) | collective-permute-done | bytes 655392 | tf_op jit(solution)/shard_map/ppermute | solution.py:13
  93.0 1.3 maximum_maximum_fusion
  94.3 1.5 fusion.31
  95.8 1.6 copy.79
  97.4 1.4 reshape.78
  98.8 54.8 %all-gather.2.cloned.1.call-done = bf16[2,2560,1280]{2,0,1:T(2,128)(2,1)} async-done(((bf16[2,20,1280]{2,0,1:T(2,128)(2,1)}), bf16[2,2560,1280]{2,0,1:T(2,128)(2,1)}) %all-gather.2.cloned.1.call-update) | async-done | bytes 13107216 | tf_op jit(solution)/shard_map/all_gather | solution.py:83
  153.6 25.4 %fusion.30 = (bf16[1,2560,1280]{2,0,1:T(2,128)(2,1)}, bf16[1,2560,1280]{2,0,1:T(2,128)(2,1)S(1)}) fusion(bf16[2,2560,1280]{2,0,1:T(2,128)(2,1)} %all-gather.2.cloned.1.call-done), kind=kLoop, calls=%fused_computation.64 | loop fusion | bytes 26214400 | tf_op jit(solution)/shard_map/slice | solution.py:85
  179.0 2.7 %fusion.6 = bf16[256,1280]{1,0:T(8,128)(2,1)} fusion(bf16[256,2560]{1,0:T(8,128)(2,1)S(1)} %copy-done.5, bf16[1,2560,1280]{2,0,1:T(2,128)(2,1)S(1)} %get-tuple-element.21), kind=kOutput, calls=%fused_computation.16 | convolution fusion | flops 1678049280 | bytes 8519680 | tf_op jit(solution)/shard_map/dot_general | solution.py:84
  181.7 1.3 copy.77
  183.1 0.3 copy.78
  183.4 8.1 %fusion.5 = bf16[256,1280]{1,0:T(8,128)(2,1)} fusion(bf16[256,2560]{1,0:T(8,128)(2,1)} %reshape.78, bf16[1,2560,1280]{2,0,1:T(2,128)(2,1)} %get-tuple-element.20), kind=kOutput, calls=%fused_computation.15 | convolution fusion | flops 1678049280 | bytes 8519680 | tf_op jit(solution)/shard_map/dot_general | solution.py:85
  191.5 1.3 copy.73
  192.8 0.6 fusion.20
  193.4 1.7 fusion.32
  195.0 0.3 fusion.11
  195.4 2.4 convolution_bitcast_fusion
  197.8 1.3 multiply_reduce_fusion
  199.1 0.9 fusion.4
  200.1 0.7 convolution_bitcast_fusion.1
  200.8 0.5 copy-done.3
  201.2 1.4 slice.53
  202.7 1.9 copy.90
  204.6 3.0 %slice.54 = f32[384,10,128]{0,2,1:T(8,128)} slice(f32[640,10,128]{0,2,1:T(8,128)} %convolution_bitcast_fusion), slice={[256:640], [0:10], [0:128]} | slice | bytes 3932160 | tf_op jit(solution)/shard_map/slice | solution.py:109
  207.6 2.9 %copy.91 = f32[1,384,1280]{2,1,0:T(8,128)} copy(f32[1,384,1280]{1,2,0:T(8,128)} %bitcast.66) | data formatting | bytes 3932160 | tf_op jit(solution)/shard_map/stack | solution.py:109
  210.5 1.3 fusion.16
  211.8 2.3 collective-permute-start.2
  214.1 15.5 %collective-permute-done.2 = bf16[2,128,1280]{2,1,0:T(8,128)(2,1)S(1)} collective-permute-done((bf16[2,128,1280]{2,1,0:T(8,128)(2,1)S(1)}, bf16[2,128,1280]{2,1,0:T(8,128)(2,1)S(1)}, u32[]{:S(2)}, u32[]{:S(2)}) %collective-permute-start.2) | collective-permute-done | bytes 655392 | tf_op jit(solution)/shard_map/ppermute | solution.py:13
  229.6 1.0 fusion.14
  230.5 2.0 collective-permute-start.3
  232.6 1.4 convolution_convert_fusion
  234.0 1.9 copy.93
  235.9 0.9 copy.92
  236.8 11.8 %collective-permute-done.3 = bf16[2,128,1280]{2,1,0:T(8,128)(2,1)} collective-permute-done((bf16[2,128,1280]{2,1,0:T(8,128)(2,1)}, bf16[2,128,1280]{2,1,0:T(8,128)(2,1)}, u32[]{:S(2)}, u32[]{:S(2)}) %collective-permute-start.3) | collective-permute-done | bytes 655392 | tf_op jit(solution)/shard_map/ppermute | solution.py:13
  248.6 1.4 fusion.18
  250.0 0.9 slice_bitcast_fusion
  (39 shorter events, 1.4 us)
Async XLA Ops:
  7.2 146.4 %all-gather.2.cloned.1.call-start = ((), (), s32[]{:S(2)}) async-start(), calls=%async_computation.1 | async-start | bytes 13209600 | tf_op jit(solution)/shard_map/all_gather | solution.py:83
  22.4 13.8 %copy-start.7 = (bf16[128,1280]{1,0:T(8,128)(2,1)S(1)}, bf16[128,1280]{1,0:T(8,128)(2,1)}, u32[]{:S(2)}) copy-start(bf16[128,1280]{1,0:T(8,128)(2,1)} %param.9) | copy-start | bytes 983044
  22.4 14.1 %copy-start.8 = (bf16[128,1280]{1,0:T(8,128)(2,1)S(1)}, bf16[128,1280]{1,0:T(8,128)(2,1)}, u32[]{:S(2)}) copy-start(bf16[128,1280]{1,0:T(8,128)(2,1)} %param.10) | copy-start | bytes 983044
  22.4 74.9 %all-to-all-start = ((bf16[128,2,2560]{2,1,0:T(2,128)(2,1)}), bf16[128,2,2560]{2,1,0:T(2,128)(2,1)S(1)}, u32[]{:S(2)}, u32[]{:S(2)}) async-start(bf16[128,2,2560]{2,1,0:T(2,128)(2,1)} %reshape.77), calls=%async_computation | async-start | bytes 2621440 | tf_op jit(solution)/shard_map/all_to_all | solution.py:75
  36.3 5.4 %copy-start.12 = (s32[16384]{0:T(1024)S(1)}, s32[16384]{0:T(1024)}, u32[]{:S(2)}) copy-start(s32[16384]{0:T(1024)} %param.14) | copy-start | bytes 196612
  36.3 5.5 %copy-start.11 = (s32[16384]{0:T(1024)S(1)}, s32[16384]{0:T(1024)}, u32[]{:S(2)}) copy-start(s32[16384]{0:T(1024)} %param.15) | copy-start | bytes 196612
  36.3 5.8 %copy-start.9 = (bf16[128,1280]{1,0:T(8,128)(2,1)S(1)}, bf16[128,1280]{1,0:T(8,128)(2,1)}, u32[]{:S(2)}) copy-start(bf16[128,1280]{1,0:T(8,128)(2,1)} %param.8) | copy-start | bytes 983044
  36.8 37.3 %collective-permute-start = (bf16[2,128,1280]{1,2,0:T(8,128)(2,1)S(1)}, bf16[2,128,1280]{1,2,0:T(8,128)(2,1)}, u32[]{:S(2)}, u32[]{:S(2)}) collective-permute-start(bf16[2,128,1280]{1,2,0:T(8,128)(2,1)S(1)} %pad_maximum_fusion.7), channel_id=1, source_target_pairs={{0,2},{2,4},{4,6},{6,8},{8,10},{10,12},{12,14},{14,16},{16,18},{18... | collective-permute-start | bytes 1966088 | tf_op jit(solution)/shard_map/ppermute | solution.py:13
  74.1 18.9 %collective-permute-start.1 = (bf16[2,128,1280]{1,2,0:T(8,128)(2,1)}, bf16[2,128,1280]{1,2,0:T(8,128)(2,1)S(1)}, u32[]{:S(2)}, u32[]{:S(2)}) collective-permute-start(bf16[2,128,1280]{1,2,0:T(8,128)(2,1)} %collective-permute-done), channel_id=1, source_target_pairs={{0,2},{2,4},{4,6},{6,8},{8,10},{10,12},{12,14},{14,16},{16,18},{18... | collective-permute-start | bytes 1966088 | tf_op jit(solution)/shard_map/ppermute | solution.py:13
  98.8 80.3 %copy-start.5 = (bf16[256,2560]{1,0:T(8,128)(2,1)S(1)}, bf16[256,2560]{1,0:T(8,128)(2,1)}, u32[]{:S(2)}) copy-start(bf16[256,2560]{1,0:T(8,128)(2,1)} %reshape.78) | copy-start | bytes 3932164
  183.4 9.4 %copy-start.1 = (bf16[256,10,128]{2,0,1:T(8,128)(2,1)}, bf16[256,10,128]{2,0,1:T(8,128)(2,1)S(1)}, u32[]{:S(2)}) copy-start(bf16[256,10,128]{2,0,1:T(8,128)(2,1)S(1)} %copy.78) | copy-start | bytes 1966084
  195.3 2.4 copy-start.6
  200.0 1.2 copy-start.3
  210.5 19.1 %copy-start = (f32[1,384,1280]{2,1,0:T(8,128)S(1)}, f32[1,384,1280]{2,1,0:T(8,128)}, u32[]{:S(2)}) copy-start(f32[1,384,1280]{2,1,0:T(8,128)} %copy.91) | copy-start | bytes 5898244
  211.8 20.8 %copy-start.2 = (bf16[256,10,128]{2,0,1:T(8,128)(2,1)S(1)}, bf16[256,10,128]{2,0,1:T(8,128)(2,1)}, u32[]{:S(2)}) copy-start(bf16[256,10,128]{2,0,1:T(8,128)(2,1)} %copy-done.1) | copy-start | bytes 1966084
  211.8 20.8 %copy-start.4 = (bf16[10,128,640]{1,2,0:T(8,128)(2,1)S(1)}, bf16[10,128,640]{1,2,0:T(8,128)(2,1)}, u32[]{:S(2)}) copy-start(bf16[10,128,640]{1,2,0:T(8,128)(2,1)} %copy-done.3) | copy-start | bytes 4915204
  211.8 17.8 %collective-permute-start.2 = (bf16[2,128,1280]{2,1,0:T(8,128)(2,1)S(1)}, bf16[2,128,1280]{2,1,0:T(8,128)(2,1)S(1)}, u32[]{:S(2)}, u32[]{:S(2)}) collective-permute-start(bf16[2,128,1280]{2,1,0:T(8,128)(2,1)S(1)} %fusion.16), channel_id=1, source_target_pairs={{2,0},{4,2},{6,4},{8,6},{10,8},{12,10},{14,12},{16,14},{18,16},{20... | collective-permute-start | bytes 1966088 | tf_op jit(solution)/shard_map/ppermute | solution.py:13
  230.5 5.4 %copy-start.10 = (bf16[10,128,128]{2,1,0:T(8,128)(2,1)S(1)}, bf16[10,128,128]{2,1,0:T(8,128)(2,1)}, u32[]{:S(2)}) copy-start(bf16[10,128,128]{2,1,0:T(8,128)(2,1)} %get-tuple-element.29) | copy-start | bytes 983044
  230.5 18.1 %collective-permute-start.3 = (bf16[2,128,1280]{2,1,0:T(8,128)(2,1)}, bf16[2,128,1280]{2,1,0:T(8,128)(2,1)}, u32[]{:S(2)}, u32[]{:S(2)}) collective-permute-start(bf16[2,128,1280]{2,1,0:T(8,128)(2,1)} %fusion.14), channel_id=1, source_target_pairs={{2,0},{4,2},{6,4},{8,6},{10,8},{12,10},{14,12},{16,14},{18,16},{20... | collective-permute-start | bytes 1966088 | tf_op jit(solution)/shard_map/ppermute | solution.py:13
Sparse Core Ops, SparseCore 0:
  11.6 141.9 all-gather.1
where the time goes:
time: 258 us
  waiting for transfers between devices  121 us (47%)
  local copies, waits for them, and re-layouts  52.4 us (20%)
  starting transfers between devices  33.3 us (13%)
  matrix products  18.3 us (7%)
  between operations  14.4 us (6%)
  blocking collectives  9.46 us (4%)
  other arithmetic  8.42 us (3%)
    ppermute x4, waiting for transfers between devices, shifted(): return lax.ppermute(value, axis, pairs)  66 us
    all_gather x1, waiting for transfers between devices, body(): piece = lax.all_gather(w_kv, 'seq', axis=1, tiled=True)  54.8 us
    slice x1, local copies, waits for them, and re-layouts, body(): proj_v = jnp.dot(source_rows, piece[1], preferred_element_type=jnp.float32)  25.4 us
    ppermute x4, starting transfers between devices, shifted(): return lax.ppermute(value, axis, pairs)  19.4 us
    all_to_all x1, starting transfers between devices, body(): lax.all_to_all(outgoing.reshape(devices, capacity, full_cache.shape[1]),...  13.8 us
    all_gather x1, blocking collectives, body(): full_cache = lax.all_gather(cache, 'head', axis=1, tiled=True)  9.46 us
    dot_general x1, matrix products, body(): proj_v = jnp.dot(source_rows, piece[1], preferred_element_type=jnp.float32)  8.07 us
  transfers between devices with their start and end apart: 6, of which 5 were waited for; matrix products, arithmetic and copies ran while one was open for 7% of the time, Pallas kernels for 0%

commit v1 on v0

v1 whole, which is shorter than its diff:
```python
import jax
import jax.numpy as jnp
from jax import lax
from jax.experimental import pallas as pl
from jax.experimental.pallas import tpu as pltpu
from jax.sharding import PartitionSpec as P

MESH = pl.DeviceIdType.MESH
NY, NX, NZ = 2, 4, 8
HD = 128
S = 128
HALF = 640
GROUPS = 5
FEAT = 1280
SLOTS = 256
NEG = -1e30
KINDS = "XZXZX"
POOL = 300


def near(offset):
    offset = offset % NZ
    return offset - NZ if offset > NZ // 2 else offset


def near_x(offset):
    offset = offset % NX
    return offset - NX if offset > NX // 2 else offset


def kernel(
    q_ref, k_ref, v_ref, g_ref, cache_ref, w_ref, doc_ref, route_ref,
    out_ref,
    rx0, wb, s_a, r_a, s_b, xb, kwb, vwb, qb, gb, bias, mem, gtx, grx, gown, stg,
    ssem, rsem, lsem,
):
    f32, bf16 = jnp.float32, jnp.bfloat16
    s = lax.axis_index("seq")
    h = lax.axis_index("head")
    c = lax.rem(s, 2)
    chip = s // 2
    z = lax.rem(chip, NZ)
    x = lax.rem(chip // NZ, NX)
    yh = chip // (NZ * NX)
    zp = lax.rem(z, 2)
    m = z // 2

    def dev(yy, xx, zz, cc, hh=None):
        return (((yy * NX + xx) * NZ + zz) * 2 + cc, h if hh is None else hh)

    def wrap(value, n):
        return lax.rem(value + 2 * n, n)

    sibling = dev(yh, x, z, 1 - c)
    other_head = (s, 1 - h)
    chips = NY * NX * NZ
    next_chip = lax.rem(chip + 1, chips)
    prev_chip = lax.rem(chip + chips - 1, chips)
    up = {"z+": dev(yh, x, wrap(z + 1, NZ), c), "z-": dev(yh, x, wrap(z - 1, NZ), c),
          "x+": dev(yh, wrap(x + 1, NX), z, c), "x-": dev(yh, wrap(x - 1, NX), z, c)}

    ids = {}
    sends = []

    def number(key):
        return ids.setdefault(key, len(ids))

    def send(key, src, dst, target):
        n = number(key)
        copy = pltpu.make_async_remote_copy(
            src_ref=src, dst_ref=dst, send_sem=ssem.at[n], recv_sem=rsem.at[n],
            device_id=target, device_id_type=MESH)
        copy.start()
        sends.append(copy)

    def recv(key, dst):
        n = number(key)
        pltpu.make_async_remote_copy(
            src_ref=dst, dst_ref=dst, send_sem=ssem.at[n], recv_sem=rsem.at[n],
            device_id=sibling, device_id_type=MESH).wait_recv()

    locals_ = []

    def local(src, dst):
        copy = pltpu.make_async_copy(src, dst, lsem.at[len(locals_)])
        copy.start()
        locals_.append(copy)
        return copy

    flips = [(a, b, d) for a in (0, 1) for b in (0, 1) for d in (0, 1) if a or b or d]
    rests = [(a, b, d) for a in (0, 1) for b in range(NX) for d in (0, 1) if a or b or d]

    barrier = pltpu.get_barrier_semaphore()
    greeted = [dev(wrap(yh + a, 2), x, 2 * m + wrap(zp + b, 2), wrap(c + d, 2)) for a, b, d in flips]
    greeted += [dev(yh, x, wrap(z + d, NZ), c) for d in range(1, NZ)]
    greeted += [dev(wrap(yh + a, 2), wrap(x + b, NX), z, wrap(c + d, 2)) for a, b, d in rests]
    greeted += [other_head]
    greeted += [(prev_chip * 2 + c, h), (prev_chip * 2 + 1 - c, h), (next_chip * 2 + c, h), (next_chip * 2 + 1 - c, h)]
    for target in greeted:
        pl.semaphore_signal(barrier, inc=1, device_id=target, device_id_type=MESH)
    pl.semaphore_wait(barrier, len(greeted))

    def cols(core):
        return pl.ds(pl.multiple_of(core * HALF, HD), HALF)

    def seg(index):
        return pl.ds(pl.multiple_of(index * S, S), S)

    mine = yh * 4 + zp * 2 + c
    for a, b, d in flips:
        zt, ct = wrap(zp + b, 2), wrap(c + d, 2)
        send(("p", a, b, d), w_ref.at[zt, :, cols(ct)], rx0.at[mine],
             dev(wrap(yh + a, 2), x, 2 * m + zt, ct))
    own_w = local(w_ref.at[zp, :, cols(c)], rx0.at[mine])

    route_own = route_ref[pl.ds(s, 1), :].astype(f32)
    row_i = lax.broadcasted_iota(jnp.int32, (S, S), 0)
    col_i = lax.broadcasted_iota(jnp.int32, (S, S), 1)
    route_col = jnp.sum(jnp.where(row_i == col_i, route_own, 0.0), axis=1, keepdims=True)
    same = (route_col == route_own) & (row_i < col_i)
    rank = jnp.sum(jnp.where(same, 1.0, 0.0), axis=0, keepdims=True)
    slot = lax.broadcasted_iota(jnp.int32, (SLOTS, S), 0)
    slot_z, slot_rest = slot // 32, lax.rem(slot // 2, 16)
    slot_dest = ((slot_rest // 2) * NZ + slot_z) * 2 + lax.rem(slot_rest, 2)
    chosen = (route_own == slot_dest.astype(f32)) & (rank == lax.rem(slot, 2).astype(f32))
    pick = jnp.where(chosen, 1.0, 0.0).astype(bf16)
    packed = jnp.dot(pick, cache_ref[...], preferred_element_type=f32).astype(bf16)
    s_a[...] = packed.reshape(NZ, 32, FEAT)
    for d in (4, 3, 5, 2, 6, 1, 7):
        zt = wrap(z + d, NZ)
        send(("a", d), s_a.at[zt], r_a.at[z], dev(yh, x, zt, c))
    own_a = local(s_a.at[z], r_a.at[z])

    def piece(g, xo, dz, part=None):
        zz = wrap(z + dz, NZ)
        xx = wrap(x + xo, NX)
        kv, mm = lax.rem(zz, 2), zz // 2
        if part is None:
            return wb.at[g, kv, :, xx, mm]
        return wb.at[g, kv, part, xx, mm]

    def pass_on(g, way, xo, dz, part=None):
        there_x = near_x(xo - {"x+": 1, "x-": -1}.get(way, 0))
        there_z = near(dz - {"z+": 1, "z-": -1}.get(way, 0))
        there = piece(g, xo, dz, part)
        send(("w", g, there_x, there_z, part), there, there, up[way])

    def got(g, xo, dz, part=None):
        recv(("w", g, xo, dz, part), piece(g, xo, dz, part))

    own_w.wait()
    for a, b, d in flips:
        source = wrap(yh + a, 2) * 4 + wrap(zp + b, 2) * 2 + wrap(c + d, 2)
        recv(("p", a, b, d), rx0.at[source])
    for y in range(2):
        block = jnp.concatenate([rx0[y * 4 + i].astype(f32) for i in range(4)], axis=0).astype(bf16)
        for g in range(GROUPS):
            wb[g, zp, y, x, m] = block[:, g * HD : (g + 1) * HD]

    for g in range(GROUPS):
        for way in ("x+", "x-", "z+", "z-"):
            pass_on(g, way, 0, 0)

    for name, ref, buf, segs in (("k", k_ref, kwb, True), ("v", v_ref, vwb, True), ("q", q_ref, qb, False), ("g", g_ref, gb, False)):
        base = 2 if segs else 0
        send((name, "s"), ref.at[:, cols(1 - c)], buf.at[seg(base + c)], sibling)
        local(ref.at[:, cols(c)], buf.at[seg(base + c)])
        if segs:
            for d in (0, 1):
                ct = wrap(c + d, 2)
                send((name, d), ref.at[:, cols(ct)], buf.at[seg(c)], (next_chip * 2 + ct, h))
    own_kv = list(locals_[2:])

    x_chunks = [g for g in range(GROUPS) if KINDS[g] == "X"]
    z_chunks = [g for g in range(GROUPS) if KINDS[g] == "Z"]

    def x_first(g, d):
        for sign, ahead in ((-1, "z+"), (1, "z-")):
            got(g, 0, sign * d)
            if d < 3:
                pass_on(g, ahead, 0, sign * d)
            else:
                pass_on(g, ahead, 0, sign * d, 0 if sign < 0 else 1)
            pass_on(g, "x+", 0, sign * d)
            pass_on(g, "x-", 0, sign * d)

    def x_first_last(g):
        got(g, 0, 4, 0)
        got(g, 0, 4, 1)
        pass_on(g, "x+", 0, 4)
        pass_on(g, "x-", 0, 4)

    def z_first(g):
        for sign, ahead in ((-1, "x+"), (1, "x-")):
            got(g, sign, 0)
            pass_on(g, ahead, sign, 0, 0 if sign < 0 else 1)
            pass_on(g, "z+", sign, 0)
            pass_on(g, "z-", sign, 0)

    def z_first_last(g):
        got(g, 2, 0, 0)
        got(g, 2, 0, 1)
        pass_on(g, "z+", 2, 0)
        pass_on(g, "z-", 2, 0)

    order = (0, -1, 1, -2, 2, -3, 3, 4)

    def x_last(g, lo, hi):
        for i in range(lo, hi):
            dz = order[i]
            got(g, -1, dz)
            if i % 2 == 0:
                pass_on(g, "x+", -1, dz)
            got(g, 1, dz)
            if i % 2 == 1:
                pass_on(g, "x-", 1, dz)

    def x_end(g):
        for dz in order:
            got(g, 2, dz)

    def z_last(g, d):
        for xo in (0, -1, 1, 2):
            for sign, ahead in ((-1, "z+"), (1, "z-")):
                got(g, xo, sign * d)
                if d < 3 or (xo in (0, -1)) == (sign < 0):
                    pass_on(g, ahead, xo, sign * d)

    def z_end(g):
        for xo in (0, -1, 1, 2):
            got(g, xo, 4)

    for g in range(GROUPS):
        if KINDS[g] == "X":
            x_first(g, 1)
        else:
            z_first(g)

    own_a.wait()
    for d in (4, 3, 5, 2, 6, 1, 7):
        recv(("a", d), r_a.at[wrap(z - d, NZ)])
    new_i = lax.broadcasted_iota(jnp.int32, (SLOTS, SLOTS), 0)
    old_i = lax.broadcasted_iota(jnp.int32, (SLOTS, SLOTS), 1)
    wanted = lax.rem(new_i // 2, NZ) * 32 + (new_i // 16) * 2 + lax.rem(new_i, 2)
    turn = jnp.where(old_i == wanted, 1.0, 0.0).astype(bf16)
    turned = jnp.dot(turn, r_a[...].reshape(SLOTS, FEAT), preferred_element_type=f32).astype(bf16)
    s_b[...] = turned.reshape(16, 16, FEAT)
    rest = (yh * NX + x) * 2 + c

    def x_rows(core, index):
        return pl.ds(pl.multiple_of(core * SLOTS + index * 16, 16), 16)

    for a, b, d in rests:
        yt, xt, ct = wrap(yh + a, 2), wrap(x + b, NX), wrap(c + d, 2)
        send(("b", a, b, d), s_b.at[(yt * NX + xt) * 2 + ct], xb.at[h, x_rows(ct, rest)], dev(yt, xt, z, ct))
    own_b = local(s_b.at[rest], xb.at[h, x_rows(c, rest)])

    for d in (2, 3):
        for g in x_chunks:
            x_first(g, d)
        if d == 2:
            for g in z_chunks:
                z_first_last(g)
    for g in x_chunks:
        x_first_last(g)

    diag = row_i == col_i
    dest_iota = lax.broadcasted_iota(jnp.int32, (S, SLOTS), 0)
    slot_iota = lax.broadcasted_iota(jnp.int32, (S, SLOTS), 1)
    slot_src = ((slot_iota // 32) * NZ + lax.rem(slot_iota // 2, NZ)) * 2 + lax.rem(slot_iota // 16, 2)
    spread = jnp.where(dest_iota == slot_src, 1.0, 0.0).astype(bf16)
    ones = jnp.ones((8, S), bf16)
    slot_no = lax.rem(lax.broadcasted_iota(jnp.int32, (1, SLOTS), 1), 2).astype(f32)
    for b in range(2):
        named = jnp.where(route_ref[...] == chip * 2 + b, 1.0, 0.0).astype(bf16)
        counts = lax.dot_general(ones, named, (((1,), (1,)), ((), ())), preferred_element_type=f32)
        by_slot = jnp.dot(counts.astype(bf16), spread, preferred_element_type=f32)[0:1]
        bias[b, :, 0:SLOTS] = jnp.broadcast_to(jnp.where(by_slot > slot_no, 0.0, NEG), (S, SLOTS))
        q_ids = doc_ref[pl.ds(chip * 2 + b, 1), :].astype(f32)
        q_col = jnp.sum(jnp.where(diag, q_ids, 0.0), axis=1, keepdims=True)
        for j in range(3):
            index = chip * 2 + b - 2 + j
            k_ids = doc_ref[pl.ds(jnp.maximum(index, 0), 1), :].astype(f32)
            k_ids = jnp.where(index >= 0, k_ids, -1.0)
            fits = q_col == k_ids
            if j == 2:
                fits = fits & (col_i <= row_i)
            bias[b, :, SLOTS + j * S : SLOTS + (j + 1) * S] = jnp.where(fits, 0.0, NEG)

    own_b.wait()
    for a, b, d in rests:
        recv(("b", a, b, d), xb.at[h, x_rows(c, (wrap(yh + a, 2) * NX + wrap(x - b, NX)) * 2 + wrap(c + d, 2))])

    def part_rows(core, i):
        return pl.ds(pl.multiple_of(core * SLOTS + i * 64, 64), 64)

    for i in range(4):
        here = xb.at[h, part_rows(c, i)]
        send(("h", i), here, here, other_head)
    for i in range(4):
        here = xb.at[h, part_rows(c, i)]
        send(("s", i), here, here, sibling)

    x_last(0, 0, 8)
    z_last(1, 1)
    z_last(1, 2)
    for i in range(4):
        here = xb.at[1 - h, part_rows(c, i)]
        recv(("h", i), here)
        send(("t", i), here, here, sibling)
    x_end(0)
    z_last(1, 3)
    x_last(2, 0, 8)
    z_end(1)
    for i in range(4):
        recv(("s", i), xb.at[h, part_rows(1 - c, i)])
        recv(("t", i), xb.at[1 - h, part_rows(1 - c, i)])
    for copy in own_kv:
        copy.wait()
    recv(("k", "s"), kwb.at[seg(3 - c)])
    recv(("v", "s"), vwb.at[seg(3 - c)])
    recv(("q", "s"), qb.at[seg(1 - c)])
    recv(("g", "s"), gb.at[seg(1 - c)])
    for d in (0, 1):
        recv(("k", d), kwb.at[seg(wrap(c + d, 2))])
        recv(("v", d), vwb.at[seg(wrap(c + d, 2))])

    nt = (((1,), (1,)), ((), ()))
    tn = (((0,), (0,)), ((), ()))
    scaling = HD ** -0.5

    def project(g):
        total = None
        for y in range(2):
            both = jnp.concatenate(
                [wb[g, kv, y].reshape(FEAT, HD) for kv in range(2)], axis=1)
            term = jnp.dot(xb[y], both, preferred_element_type=f32)
            total = term if total is None else total + term
        mem[0] = total[:, :HD].astype(bf16)
        mem[1] = total[:, HD:].astype(bf16)

    def attend(g):
        lanes = slice(g * HD, (g + 1) * HD)
        for b in range(2):
            rows = slice(b * S, (b + 1) * S)
            window = slice(b * S, b * S + 3 * S)
            query, cot = qb[rows, lanes], gb[rows, lanes]
            keys = jnp.concatenate([mem[0, b * SLOTS : (b + 1) * SLOTS], kwb[window, lanes]], axis=0)
            vals = jnp.concatenate([mem[1, b * SLOTS : (b + 1) * SLOTS], vwb[window, lanes]], axis=0)
            scores = lax.dot_general(query, keys, nt, preferred_element_type=f32) * scaling + bias[b]
            top = jnp.max(scores, axis=1, keepdims=True)
            weights = jnp.exp(scores - top)
            prob = weights * (1.0 / jnp.sum(weights, axis=1, keepdims=True))
            prob_b = prob.astype(bf16)
            out = jnp.dot(prob_b, vals, preferred_element_type=f32).astype(bf16)
            dprob = lax.dot_general(cot, vals, nt, preferred_element_type=f32)
            delta = jnp.sum(cot.astype(f32) * out.astype(f32), axis=1, keepdims=True)
            dscore = (prob * (dprob - delta) * scaling).astype(bf16)
            grad_q = jnp.dot(dscore, keys, preferred_element_type=f32).astype(bf16)
            stg[0, b, :, lanes] = out
            stg[1, b, :, lanes] = grad_q
            grad_k = lax.dot_general(dscore[:, SLOTS:], query, tn, preferred_element_type=f32)
            grad_v = lax.dot_general(prob_b[:, SLOTS:], cot, tn, preferred_element_type=f32)
            for i, grad in enumerate((grad_k, grad_v)):
                if b == 0:
                    gown[g, i, 0 : 3 * S] = grad
                else:
                    gown[g, i, S : 3 * S] += grad[: 2 * S]
                    gown[g, i, 3 * S :] = grad[2 * S :]
        for i in range(2):
            gtx[g, i] = gown[g, i, : 2 * S].astype(bf16)
        send(("e", g), gtx.at[g], grx.at[g], (prev_chip * 2 + c, h))
        hand_over(g, 0)

    def hand_over(g, first):
        lanes = pl.ds(g * HD, HD)
        there = out_ref.at[pl.ds(first, 2), :, pl.ds(pl.multiple_of(c * HALF + g * HD, HD), HD)]
        send(("o", g, first), stg.at[pl.ds(first, 2), 1 - c, :, lanes], there, sibling)
        local(stg.at[pl.ds(first, 2), c, :, lanes], there)

    def finish(g):
        lanes = slice(g * HD, (g + 1) * HD)
        recv(("e", g), grx.at[g])
        for i in range(2):
            total = (gown[g, i, 2 * S :] + grx[g, i].astype(f32)).astype(bf16)
            for b in range(2):
                stg[2 + i, b, :, lanes] = total[b * S : (b + 1) * S]
        hand_over(g, 2)

    project(0)
    z_last(3, 1)
    x_last(4, 0, 4)
    attend(0)
    z_last(3, 2)
    x_last(4, 4, 8)
    project(1)
    x_end(2)
    z_last(3, 3)
    attend(1)
    project(2)
    attend(2)
    finish(0)
    z_end(3)
    project(3)
    attend(3)
    finish(1)
    finish(2)
    x_end(4)
    project(4)
    attend(4)
    finish(3)
    finish(4)
    for g in range(GROUPS):
        for first in (0, 2):
            recv(("o", g, first), out_ref.at[
                pl.ds(first, 2), :, pl.ds(pl.multiple_of((1 - c) * HALF + g * HD, HD), HD)])
    for copy in locals_[len(own_kv) + 3 :]:
        copy.wait()
    for copy in sends:
        copy.wait_send()
    assert len(ids) <= POOL


def body(queries, keys, values, grad_out, cache, w_kv, doc_ids, routes):
    bf16, f32 = jnp.bfloat16, jnp.float32
    vmem = pl.BlockSpec(memory_space=pltpu.VMEM)
    result = pl.pallas_call(
        kernel,
        out_shape=jax.ShapeDtypeStruct((4, S, FEAT), bf16),
        in_specs=[vmem] * 8,
        out_specs=vmem,
        scratch_shapes=[
            pltpu.VMEM((8, 20, HALF), bf16),
            pltpu.VMEM((GROUPS, 2, NY, NX, NZ // 2, 80, HD), bf16),
            pltpu.VMEM((NZ, 32, FEAT), bf16),
            pltpu.VMEM((NZ, 32, FEAT), bf16),
            pltpu.VMEM((16, 16, FEAT), bf16),
            pltpu.VMEM((2, 2 * SLOTS, FEAT), bf16),
            pltpu.VMEM((4 * S, HALF), bf16),
            pltpu.VMEM((4 * S, HALF), bf16),
            pltpu.VMEM((2 * S, HALF), bf16),
            pltpu.VMEM((2 * S, HALF), bf16),
            pltpu.VMEM((2, S, SLOTS + 3 * S), f32),
            pltpu.VMEM((2, 2 * SLOTS, HD), bf16),
            pltpu.VMEM((GROUPS, 2, 2 * S, HD), bf16),
            pltpu.VMEM((GROUPS, 2, 2 * S, HD), bf16),
            pltpu.VMEM((GROUPS, 2, 4 * S, HD), f32),
            pltpu.VMEM((4, 2, S, HALF), bf16),
            pltpu.SemaphoreType.DMA((POOL,)),
            pltpu.SemaphoreType.DMA((POOL,)),
            pltpu.SemaphoreType.DMA((24,)),
        ],
        compiler_params=pltpu.CompilerParams(
            collective_id=0, has_side_effects=True, vmem_limit_bytes=50 * 2**20
        ),
        name="segment_layer",
    )(queries, keys, values, grad_out, cache, w_kv, doc_ids.reshape(S, S), routes.reshape(S, S))
    return (result[0], result[1], result[2], result[3])


def solution(mesh):
    rows = P("seq", "head")
    return jax.shard_map(
        body,
        mesh=mesh,
        in_specs=(rows, rows, rows, rows, rows, P(None, "seq", "head"), P(), P()),
        out_specs=(rows, rows, rows, rows),
        check_vma=False,
    )
```

time: 258 us -> 127 us (0.49)
  the two profiles are of different devices: /device:TPU:231 before, /device:TPU:1 now
where the time goes in v1:
time: 127 us
  Pallas kernels  117 us (92%)
  local copies, waits for them, and re-layouts  8.51 us (7%)
    pallas_call x1, Pallas kernels, body(): pl.pallas_call(kernel, out_shape=jax.ShapeDtypeStruct((4, S, FEAT), bf16)...  117 us
    unnamed x15, local copies, waits for them, and re-layouts  7.44 us

profile of v1, /device:TPU:1, one launch (start us, length us, event | category | flops | bytes accessed | tf_op | source)
XLA Modules:
  0.0 126.6 jit_solution(17036813629527007513)
XLA Ops:
  0.6 0.9 copy.12.w_ref
  1.5 0.0 copy-start
  1.6 1.0 copy-done
  2.5 0.0 copy-start.1
  2.5 1.0 copy-done.1
  3.5 0.0 copy-start.2
  3.5 1.0 copy-done.2
  4.5 0.0 copy-start.3
  4.5 1.0 copy-done.3
  5.4 0.0 copy-start.4
  5.4 1.0 copy-done.4
  6.4 0.0 copy-start.5
  6.4 0.8 copy-done.5
  7.3 0.0 copy-start.6
  7.3 0.8 copy-done.6
  8.1 117.4 %segment_layer.1 = bf16[4,128,1280]{2,1,0:T(8,128)(2,1)S(1)} custom-call(bf16[128,1280]{1,0:T(8,128)(2,1)S(1)} %copy-done, bf16[128,1280]{1,0:T(8,128)(2,1)S(1)} %copy-done.1, bf16[128,1280]{1,0:T(8,128)(2,1)S(1)} %copy-done.2, bf16[128,1280]{1,0:T(8,128)(2,1)S(1)} %copy-done.3, bf16[128,1280]{1,0:T(8,128)(2,1)S(1)} %copy-done.4, ...), custom_call_target="tpu_custom_call" | custom-call | tf_op jit(solution)/shard_map/segment_layer/pallas_call | solution.py:427
  125.5 1.1 slice_bitcast_fusion
Async XLA Ops:
  1.5 1.0 copy-start
  2.5 1.0 copy-start.1
  3.5 1.0 copy-start.2
  4.5 1.0 copy-start.3
  5.4 1.0 copy-start.4
  6.4 0.8 copy-start.5
  7.3 0.8 copy-start.6

commit v2 on v1

v2 whole, which is shorter than its diff:
```python
import jax
import jax.numpy as jnp
from jax import lax
from jax.experimental import pallas as pl
from jax.experimental.pallas import tpu as pltpu
from jax.sharding import PartitionSpec as P

MESH = pl.DeviceIdType.MESH
NY, NX, NZ = 2, 4, 8
HD = 128
S = 128
HALF = 640
GROUPS = 5
FEAT = 1280
SLOTS = 256
NEG = -1e30
KINDS = "XZXXX"
CHUNKS = ((0, 512), (512, 512), (1024, 256))
POOL = 340


def near(offset):
    offset = offset % NZ
    return offset - NZ if offset > NZ // 2 else offset


def near_x(offset):
    offset = offset % NX
    return offset - NX if offset > NX // 2 else offset


def kernel(
    q_ref, k_ref, v_ref, g_ref, cache_ref, w_ref, doc_ref, route_ref,
    out_ref,
    routes, docs, held, rx0, wb, s_b, r_b, s_a, xb, kwb, vwb, qb, gb, bias, mem, gtx, grx, gown, stg,
    ssem, rsem, lsem,
):
    f32, bf16 = jnp.float32, jnp.bfloat16
    s = lax.axis_index("seq")
    h = lax.axis_index("head")
    c = lax.rem(s, 2)
    chip = s // 2
    z = lax.rem(chip, NZ)
    x = lax.rem(chip // NZ, NX)
    yh = chip // (NZ * NX)
    zp = lax.rem(z, 2)
    m = z // 2

    def dev(yy, xx, zz, cc, hh=None):
        return (((yy * NX + xx) * NZ + zz) * 2 + cc, h if hh is None else hh)

    def wrap(value, n):
        return lax.rem(value + 2 * n, n)

    sibling = dev(yh, x, z, 1 - c)
    other_head = (s, 1 - h)
    chips = NY * NX * NZ
    next_chip = lax.rem(chip + 1, chips)
    prev_chip = lax.rem(chip + chips - 1, chips)
    up = {"z+": dev(yh, x, wrap(z + 1, NZ), c), "z-": dev(yh, x, wrap(z - 1, NZ), c),
          "x+": dev(yh, wrap(x + 1, NX), z, c), "x-": dev(yh, wrap(x - 1, NX), z, c)}

    ids = {}
    sends = []

    def number(key):
        return ids.setdefault(key, len(ids))

    def send(key, src, dst, target):
        n = number(key)
        copy = pltpu.make_async_remote_copy(
            src_ref=src, dst_ref=dst, send_sem=ssem.at[n], recv_sem=rsem.at[n],
            device_id=target, device_id_type=MESH)
        copy.start()
        sends.append(copy)

    def recv(key, dst):
        n = number(key)
        pltpu.make_async_remote_copy(
            src_ref=dst, dst_ref=dst, send_sem=ssem.at[n], recv_sem=rsem.at[n],
            device_id=sibling, device_id_type=MESH).wait_recv()

    locals_ = []

    def local(src, dst):
        copy = pltpu.make_async_copy(src, dst, lsem.at[len(locals_)])
        copy.start()
        locals_.append(copy)
        return copy

    flips = [(a, b, d) for a in (0, 1) for b in (0, 1) for d in (0, 1) if a or b or d]
    planes = [(a, b) for a, b in ((1, 2), (0, 2), (1, 1), (1, 3), (1, 0), (0, 1), (0, 3))]

    route_load = local(route_ref, routes)
    doc_load = local(doc_ref, docs)
    held_load = local(cache_ref, held)

    barrier = pltpu.get_barrier_semaphore()
    greeted = [dev(wrap(yh + a, 2), x, 2 * m + wrap(zp + b, 2), wrap(c + d, 2)) for a, b, d in flips]
    greeted += [dev(yh, x, wrap(z + d, NZ), c) for d in range(1, NZ)]
    greeted += [dev(wrap(yh + a, 2), wrap(x + b, NX), z, c) for a, b in planes]
    greeted += [other_head]
    greeted += [(prev_chip * 2 + c, h), (prev_chip * 2 + 1 - c, h), (next_chip * 2 + c, h), (next_chip * 2 + 1 - c, h)]
    for target in greeted:
        pl.semaphore_signal(barrier, inc=1, device_id=target, device_id_type=MESH)

    def cols(core):
        return pl.ds(pl.multiple_of(core * HALF, HD), HALF)

    def seg(index):
        return pl.ds(pl.multiple_of(index * S, S), S)

    route_load.wait()
    route_own = routes[pl.ds(s, 1), :].astype(f32)
    row_i = lax.broadcasted_iota(jnp.int32, (S, S), 0)
    col_i = lax.broadcasted_iota(jnp.int32, (S, S), 1)
    route_col = jnp.sum(jnp.where(row_i == col_i, route_own, 0.0), axis=1, keepdims=True)
    same = (route_col == route_own) & (row_i < col_i)
    rank = jnp.sum(jnp.where(same, 1.0, 0.0), axis=0, keepdims=True)
    slot = lax.broadcasted_iota(jnp.int32, (SLOTS, S), 0)
    chosen = (route_own == (slot // 2).astype(f32)) & (rank == lax.rem(slot, 2).astype(f32))
    pick = jnp.where(chosen, 1.0, 0.0).astype(bf16)

    pl.semaphore_wait(barrier, len(greeted))

    mine = yh * 4 + zp * 2 + c
    for a, b, d in flips:
        zt, ct = wrap(zp + b, 2), wrap(c + d, 2)
        send(("p", a, b, d), w_ref.at[zt, :, cols(ct)], rx0.at[mine],
             dev(wrap(yh + a, 2), x, 2 * m + zt, ct))
    own_w = local(w_ref.at[zp, :, cols(c)], rx0.at[mine])

    held_load.wait()
    plane = yh * NX + x
    own_b = []
    for i, (first, count) in enumerate(CHUNKS):
        lanes = slice(first, first + count)
        packed = jnp.dot(pick, held[:, lanes], preferred_element_type=f32).astype(bf16)
        s_b[:, :, lanes] = packed.reshape(NY * NX, 32, count)
        lanes = pl.ds(first, count)
        for a, b in planes:
            yt, xt = wrap(yh + a, 2), wrap(x + b, NX)
            send(("b", i, a, b), s_b.at[yt * NX + xt, :, lanes], r_b.at[plane, :, lanes], dev(yt, xt, z, c))
        own_b.append(local(s_b.at[plane, :, lanes], r_b.at[plane, :, lanes]))

    def piece(g, xo, dz, part=None):
        zz = wrap(z + dz, NZ)
        xx = wrap(x + xo, NX)
        kv, mm = lax.rem(zz, 2), zz // 2
        if KINDS[g] in "PQ":
            return wb.at[g, kv, yh, xx, mm]
        if part is None:
            return wb.at[g, kv, :, xx, mm]
        return wb.at[g, kv, part, xx, mm]

    def pass_on(g, way, xo, dz, part=None):
        there_x = near_x(xo - {"x+": 1, "x-": -1}.get(way, 0))
        there_z = near(dz - {"z+": 1, "z-": -1}.get(way, 0))
        there = piece(g, xo, dz, part)
        send(("w", g, there_x, there_z, part), there, there, up[way])

    def got(g, xo, dz, part=None):
        recv(("w", g, xo, dz, part), piece(g, xo, dz, part))
        if KINDS[g] in "PQ":
            cross(g, xo, dz)

    def cross(g, xo, dz):
        there = piece(g, xo, dz)
        send(("y", g, xo, dz), there, there, dev(1 - yh, x, z, c))

    def crossed(g, xo, dz):
        zz = wrap(z + dz, NZ)
        recv(("y", g, xo, dz), wb.at[g, lax.rem(zz, 2), 1 - yh, wrap(x + xo, NX), zz // 2])

    def crossed_all(g):
        if KINDS[g] not in "PQ":
            return
        for xo in (0, -1, 1, 2):
            for dz in order:
                crossed(g, xo, dz)

    own_w.wait()
    for a, b, d in flips:
        source = wrap(yh + a, 2) * 4 + wrap(zp + b, 2) * 2 + wrap(c + d, 2)
        recv(("p", a, b, d), rx0.at[source])
    for y in range(2):
        block = jnp.concatenate([rx0[y * 4 + i].astype(f32) for i in range(4)], axis=0).astype(bf16)
        for g in range(GROUPS):
            wb[g, zp, y, x, m] = block[:, g * HD : (g + 1) * HD]

    for g in range(GROUPS):
        for way in ("x+", "x-", "z+", "z-"):
            pass_on(g, way, 0, 0)
        if KINDS[g] in "PQ":
            cross(g, 0, 0)

    order = (0, -1, 1, -2, 2, -3, 3, 4)

    def x_first(g, d):
        whole = KINDS[g] == "P"
        for sign, ahead in ((-1, "z+"), (1, "z-")):
            got(g, 0, sign * d)
            if d < 3:
                pass_on(g, ahead, 0, sign * d)
            elif not whole:
                pass_on(g, ahead, 0, sign * d, 0 if sign < 0 else 1)
            elif sign < 0:
                pass_on(g, ahead, 0, sign * d)
            pass_on(g, "x+", 0, sign * d)
            pass_on(g, "x-", 0, sign * d)

    def x_first_last(g):
        if KINDS[g] == "P":
            got(g, 0, 4)
        else:
            got(g, 0, 4, 0)
            got(g, 0, 4, 1)
        pass_on(g, "x+", 0, 4)
        pass_on(g, "x-", 0, 4)

    def z_first(g):
        for sign, ahead in ((-1, "x+"), (1, "x-")):
            got(g, sign, 0)
            if sign < 0:
                pass_on(g, ahead, sign, 0)
            pass_on(g, "z+", sign, 0)
            pass_on(g, "z-", sign, 0)

    def z_first_last(g):
        got(g, 2, 0)
        pass_on(g, "z+", 2, 0)
        pass_on(g, "z-", 2, 0)

    def x_last(g, lo, hi):
        for i in range(lo, hi):
            dz = order[i]
            got(g, -1, dz)
            if i % 2 == 0:
                pass_on(g, "x+", -1, dz)
            got(g, 1, dz)
            if i % 2 == 1:
                pass_on(g, "x-", 1, dz)

    def x_end(g):
        for dz in order:
            got(g, 2, dz)

    def z_last(g, d):
        for xo in (0, -1, 1, 2):
            for sign, ahead in ((-1, "z+"), (1, "z-")):
                got(g, xo, sign * d)
                if d < 3 or (xo in (0, -1)) == (sign < 0):
                    pass_on(g, ahead, xo, sign * d)

    def z_end(g):
        for xo in (0, -1, 1, 2):
            got(g, xo, 4)

    def last(g, stage):
        if KINDS[g] in "XP":
            if stage < 3:
                x_last(g, (0, 3, 6)[stage], (3, 6, 8)[stage])
            else:
                x_end(g)
        elif stage < 3:
            z_last(g, stage + 1)
        else:
            z_end(g)

    x_chunks = [g for g in range(GROUPS) if KINDS[g] in "XP"]
    z_chunks = [g for g in range(GROUPS) if KINDS[g] in "QZ"]
    for g in x_chunks:
        x_first(g, 1)
    for g in z_chunks:
        z_first(g)

    new_i = lax.broadcasted_iota(jnp.int32, (SLOTS, SLOTS), 0)
    old_i = lax.broadcasted_iota(jnp.int32, (SLOTS, SLOTS), 1)
    wanted = lax.rem(new_i // 2, 8) * 32 + (new_i // 16) * 2 + lax.rem(new_i, 2)
    turn = jnp.where(old_i == wanted, 1.0, 0.0).astype(bf16)
    own_a = []
    for i, (first, count) in enumerate(CHUNKS):
        lanes = slice(first, first + count)
        own_b[i].wait()
        for a, b in planes:
            recv(("b", i, a, b), r_b.at[wrap(yh + a, 2) * NX + wrap(x - b, NX), :, pl.ds(first, count)])
        old = r_b[:, :, lanes].reshape(SLOTS, count)
        s_a[:, :, lanes] = jnp.dot(turn, old, preferred_element_type=f32).astype(bf16).reshape(NZ, 32, count)
        lanes = pl.ds(first, count)
        for d in (4, 3, 5, 2, 6, 1, 7):
            zt = wrap(z + d, NZ)
            send(("a", i, d), s_a.at[zt, :, lanes], xb.at[h, c, z, :, lanes], dev(yh, x, zt, c))
        own_a.append(local(s_a.at[z, :, lanes], xb.at[h, c, z, :, lanes]))

    for g in x_chunks:
        x_first(g, 2)
    for g in z_chunks:
        z_first_last(g)

    for g in x_chunks:
        x_first(g, 3)
    for g in x_chunks:
        x_first_last(g)

    doc_load.wait()
    diag = row_i == col_i
    src_iota = lax.broadcasted_iota(jnp.int32, (S, SLOTS), 0)
    slot_iota = lax.broadcasted_iota(jnp.int32, (S, SLOTS), 1)
    slot_src = (lax.rem(slot_iota // 2, 8) * NZ + lax.rem(slot_iota // 16, NZ)) * 2 + slot_iota // S
    spread = jnp.where(src_iota == slot_src, 1.0, 0.0).astype(bf16)
    ones = jnp.ones((8, S), bf16)
    slot_no = lax.rem(lax.broadcasted_iota(jnp.int32, (1, SLOTS), 1), 2).astype(f32)
    for b in range(2):
        named = jnp.where(routes[...] == chip * 2 + b, 1.0, 0.0).astype(bf16)
        counts = lax.dot_general(ones, named, (((1,), (1,)), ((), ())), preferred_element_type=f32)
        by_slot = jnp.dot(counts.astype(bf16), spread, preferred_element_type=f32)[0:1]
        bias[b, :, 0:SLOTS] = jnp.broadcast_to(jnp.where(by_slot > slot_no, 0.0, NEG), (S, SLOTS))
        q_ids = docs[pl.ds(chip * 2 + b, 1), :].astype(f32)
        q_col = jnp.sum(jnp.where(diag, q_ids, 0.0), axis=1, keepdims=True)
        for j in range(3):
            index = chip * 2 + b - 2 + j
            k_ids = docs[pl.ds(jnp.maximum(index, 0), 1), :].astype(f32)
            k_ids = jnp.where(index >= 0, k_ids, -1.0)
            fits = q_col == k_ids
            if j == 2:
                fits = fits & (col_i <= row_i)
            bias[b, :, SLOTS + j * S : SLOTS + (j + 1) * S] = jnp.where(fits, 0.0, NEG)

    def spread_rows(i):
        lanes = pl.ds(*CHUNKS[i])
        own_a[i].wait()
        for d in (4, 3, 5, 2, 6, 1, 7):
            recv(("a", i, d), xb.at[h, c, wrap(z - d, NZ), :, lanes])
        here = xb.at[h, c, :, :, lanes]
        send(("h", i), here, here, other_head)
        send(("s", i), here, here, sibling)

    def forward_rows(i):
        here = xb.at[1 - h, c, :, :, pl.ds(*CHUNKS[i])]
        recv(("h", i), here)
        send(("t", i), here, here, sibling)

    last(0, 0)
    last(1, 0)
    spread_rows(0)
    own_kv = []
    for name, ref, buf, segs in (("k", k_ref, kwb, True), ("v", v_ref, vwb, True), ("q", q_ref, qb, False), ("g", g_ref, gb, False)):
        base = 2 if segs else 0
        send((name, "s"), ref.at[:, cols(1 - c)], buf.at[seg(base + c)], sibling)
        own_kv.append(local(ref.at[:, cols(c)], buf.at[seg(base + c)]))
        if segs:
            for d in (0, 1):
                ct = wrap(c + d, 2)
                send((name, d), ref.at[:, cols(ct)], buf.at[seg(c)], (next_chip * 2 + ct, h))

    last(0, 1)
    last(1, 1)
    spread_rows(1)
    last(0, 2)
    last(1, 2)
    spread_rows(2)
    forward_rows(0)
    last(0, 3)
    last(2, 0)
    forward_rows(1)
    last(1, 3)
    last(2, 1)
    last(3, 0)
    forward_rows(2)
    last(2, 2)
    last(3, 1)
    for i in range(len(CHUNKS)):
        lanes = pl.ds(*CHUNKS[i])
        recv(("s", i), xb.at[h, 1 - c, :, :, lanes])
        recv(("t", i), xb.at[1 - h, 1 - c, :, :, lanes])
    handed = []
    nt = (((1,), (1,)), ((), ()))
    tn = (((0,), (0,)), ((), ()))
    scaling = HD ** -0.5

    def project(g):
        total = None
        for y in range(2):
            both = jnp.concatenate(
                [wb[g, kv, y].reshape(FEAT, HD) for kv in range(2)], axis=1)
            term = jnp.dot(xb[y].reshape(2 * SLOTS, FEAT), both, preferred_element_type=f32)
            total = term if total is None else total + term
        mem[0] = total[:, :HD].astype(bf16).reshape(16, 2, 16, HD)
        mem[1] = total[:, HD:].astype(bf16).reshape(16, 2, 16, HD)

    def attend(g):
        lanes = slice(g * HD, (g + 1) * HD)
        for b in range(2):
            rows = slice(b * S, (b + 1) * S)
            window = slice(b * S, b * S + 3 * S)
            query, cot = qb[rows, lanes], gb[rows, lanes]
            keys = jnp.concatenate([mem[0, :, b].reshape(SLOTS, HD), kwb[window, lanes]], axis=0)
            vals = jnp.concatenate([mem[1, :, b].reshape(SLOTS, HD), vwb[window, lanes]], axis=0)
            scores = lax.dot_general(query, keys, nt, preferred_element_type=f32) * scaling + bias[b]
            top = jnp.max(scores, axis=1, keepdims=True)
            weights = jnp.exp(scores - top)
            prob = weights * (1.0 / jnp.sum(weights, axis=1, keepdims=True))
            prob_b = prob.astype(bf16)
            out = jnp.dot(prob_b, vals, preferred_element_type=f32).astype(bf16)
            dprob = lax.dot_general(cot, vals, nt, preferred_element_type=f32)
            delta = jnp.sum(cot.astype(f32) * out.astype(f32), axis=1, keepdims=True)
            dscore = (prob * (dprob - delta) * scaling).astype(bf16)
            grad_q = jnp.dot(dscore, keys, preferred_element_type=f32).astype(bf16)
            stg[0, b, :, lanes] = out
            stg[1, b, :, lanes] = grad_q
            grad_k = lax.dot_general(dscore[:, SLOTS:], query, tn, preferred_element_type=f32)
            grad_v = lax.dot_general(prob_b[:, SLOTS:], cot, tn, preferred_element_type=f32)
            for i, grad in enumerate((grad_k, grad_v)):
                if b == 0:
                    gown[g, i, 0 : 3 * S] = grad
                else:
                    gown[g, i, S : 3 * S] += grad[: 2 * S]
                    gown[g, i, 3 * S :] = grad[2 * S :]
        for i in range(2):
            gtx[g, i] = gown[g, i, : 2 * S].astype(bf16)
        send(("e", g), gtx.at[g], grx.at[g], (prev_chip * 2 + c, h))
        hand_over(g, 0)

    def hand_over(g, first):
        lanes = pl.ds(g * HD, HD)
        there = out_ref.at[pl.ds(first, 2), :, pl.ds(pl.multiple_of(c * HALF + g * HD, HD), HD)]
        send(("o", g, first), stg.at[pl.ds(first, 2), 1 - c, :, lanes], there, sibling)
        handed.append(local(stg.at[pl.ds(first, 2), c, :, lanes], there))

    def finish(g):
        lanes = slice(g * HD, (g + 1) * HD)
        recv(("e", g), grx.at[g])
        for i in range(2):
            total = (gown[g, i, 2 * S :] + grx[g, i].astype(f32)).astype(bf16)
            for b in range(2):
                stg[2 + i, b, :, lanes] = total[b * S : (b + 1) * S]
        hand_over(g, 2)

    crossed_all(0)
    project(0)
    last(4, 0)
    last(3, 2)
    for copy in own_kv:
        copy.wait()
    recv(("k", "s"), kwb.at[seg(3 - c)])
    recv(("v", "s"), vwb.at[seg(3 - c)])
    recv(("q", "s"), qb.at[seg(1 - c)])
    recv(("g", "s"), gb.at[seg(1 - c)])
    for d in (0, 1):
        recv(("k", d), kwb.at[seg(wrap(c + d, 2))])
        recv(("v", d), vwb.at[seg(wrap(c + d, 2))])

    attend(0)
    last(4, 1)
    last(2, 3)
    crossed_all(1)
    project(1)
    last(4, 2)
    attend(1)
    crossed_all(2)
    project(2)
    attend(2)
    finish(0)
    last(3, 3)
    crossed_all(3)
    project(3)
    attend(3)
    finish(1)
    finish(2)
    last(4, 3)
    crossed_all(4)
    project(4)
    attend(4)
    finish(3)
    finish(4)
    for g in range(GROUPS):
        for first in (0, 2):
            recv(("o", g, first), out_ref.at[
                pl.ds(first, 2), :, pl.ds(pl.multiple_of((1 - c) * HALF + g * HD, HD), HD)])
    for copy in handed:
        copy.wait()
    for copy in sends:
        copy.wait_send()
    assert len(ids) <= POOL


def body(queries, keys, values, grad_out, cache, w_kv, doc_ids, routes):
    bf16, f32 = jnp.bfloat16, jnp.float32
    vmem = pl.BlockSpec(memory_space=pltpu.VMEM)
    hbm = pl.BlockSpec(memory_space=pltpu.HBM)
    result = pl.pallas_call(
        kernel,
        out_shape=jax.ShapeDtypeStruct((4, S, FEAT), bf16),
        in_specs=[hbm] * 5 + [vmem] + [hbm] * 2,
        out_specs=vmem,
        scratch_shapes=[
            pltpu.VMEM((S, S), jnp.int32),
            pltpu.VMEM((S, S), jnp.int32),
            pltpu.VMEM((S, FEAT), bf16),
            pltpu.VMEM((8, 20, HALF), bf16),
            pltpu.VMEM((GROUPS, 2, NY, NX, NZ // 2, 80, HD), bf16),
            pltpu.VMEM((NZ, 32, FEAT), bf16),
            pltpu.VMEM((NZ, 32, FEAT), bf16),
            pltpu.VMEM((NZ, 32, FEAT), bf16),
            pltpu.VMEM((2, 2, NZ, 32, FEAT), bf16),
            pltpu.VMEM((4 * S, HALF), bf16),
            pltpu.VMEM((4 * S, HALF), bf16),
            pltpu.VMEM((2 * S, HALF), bf16),
            pltpu.VMEM((2 * S, HALF), bf16),
            pltpu.VMEM((2, S, SLOTS + 3 * S), f32),
            pltpu.VMEM((2, 16, 2, 16, HD), bf16),
            pltpu.VMEM((GROUPS, 2, 2 * S, HD), bf16),
            pltpu.VMEM((GROUPS, 2, 2 * S, HD), bf16),
            pltpu.VMEM((GROUPS, 2, 4 * S, HD), f32),
            pltpu.VMEM((4, 2, S, HALF), bf16),
            pltpu.SemaphoreType.DMA((POOL,)),
            pltpu.SemaphoreType.DMA((POOL,)),
            pltpu.SemaphoreType.DMA((32,)),
        ],
        compiler_params=pltpu.CompilerParams(
            collective_id=0, has_side_effects=True, vmem_limit_bytes=64 * 2**20
        ),
        name="segment_layer",
    )(queries, keys, values, grad_out, cache, w_kv, doc_ids.reshape(S, S), routes.reshape(S, S))
    return (result[0], result[1], result[2], result[3])


def solution(mesh):
    rows = P("seq", "head")
    return jax.shard_map(
        body,
        mesh=mesh,
        in_specs=(rows, rows, rows, rows, rows, P(None, "seq", "head"), P(), P()),
        out_specs=(rows, rows, rows, rows),
        check_vma=False,
    )
```

time: 127 us -> 119 us (0.937)
  the two profiles are of different devices: /device:TPU:1 before, /device:TPU:231 now
where the time goes in v2:
time: 119 us; the launch traced here: 117 us
  Pallas kernels  112 us (94%)
  local copies, waits for them, and re-layouts  3.9 us (3%)
    pallas_call x1, Pallas kernels, body(): pl.pallas_call(kernel, out_shape=jax.ShapeDtypeStruct((4, S, FEAT), bf16)...  112 us

profile of v2, /device:TPU:231, one launch (start us, length us, event | category | flops | bytes accessed | tf_op | source)
XLA Modules:
  0.0 116.9 jit_solution(1918687405216717941)
XLA Ops:
  0.6 1.6 %copy.12.w_ref = bf16[2,20,1280]{2,1,0:T(8,128)(2,1)} copy(bf16[2,20,1280]{2,0,1:T(2,128)(2,1)} %param.13) | data formatting | bytes 204800 | tf_op args[5]
  2.2 112.4 %segment_layer.1 = bf16[4,128,1280]{2,1,0:T(8,128)(2,1)} custom-call(bf16[128,1280]{1,0:T(8,128)(2,1)} %q_ref.1, bf16[128,1280]{1,0:T(8,128)(2,1)} %k_ref.1, bf16[128,1280]{1,0:T(8,128)(2,1)} %v_ref.1, bf16[128,1280]{1,0:T(8,128)(2,1)} %g_ref.1, bf16[128,1280]{1,0:T(8,128)(2,1)} %cache_ref.1, bf16[2,20,1280]{2,1,0:T(8,128)(2,1)} %copy.12.w_ref, ...), custom_call_target="tpu_custom_call" | custom-call | tf_op jit(solution)/shard_map/segment_layer/pallas_call | solution.py:491
  114.6 2.3 %slice_bitcast_fusion = (bf16[128,1280]{1,0:T(8,128)(2,1)}, bf16[128,1280]{1,0:T(8,128)(2,1)}, bf16[128,1280]{1,0:T(8,128)(2,1)}, bf16[128,1280]{1,0:T(8,128)(2,1)}) fusion(bf16[4,128,1280]{2,1,0:T(8,128)(2,1)} %segment_layer.1), kind=kLoop, calls=%fused_computation | loop fusion | bytes 2621440 | tf_op jit(solution)/shard_map/squeeze | solution.py:525

commit v3 on v2

--- a/solution.py
+++ b/solution.py
@@ -14,7 +14,7 @@
 FEAT = 1280
 SLOTS = 256
 NEG = -1e30
-KINDS = "XZXXX"
+KINDS = "ZXXXX"
 CHUNKS = ((0, 512), (512, 512), (1024, 256))
 POOL = 340
 
@@ -343,6 +343,9 @@
     last(0, 0)
     last(1, 0)
     spread_rows(0)
+    last(0, 1)
+    last(1, 1)
+    spread_rows(1)
     own_kv = []
     for name, ref, buf, segs in (("k", k_ref, kwb, True), ("v", v_ref, vwb, True), ("q", q_ref, qb, False), ("g", g_ref, gb, False)):
         base = 2 if segs else 0
@@ -353,9 +356,6 @@
                 ct = wrap(c + d, 2)
                 send((name, d), ref.at[:, cols(ct)], buf.at[seg(c)], (next_chip * 2 + ct, h))
 
-    last(0, 1)
-    last(1, 1)
-    spread_rows(1)
     last(0, 2)
     last(1, 2)
     spread_rows(2)

time: 119 us -> 120 us (level)
  Pallas kernels: 112 us -> 114 us
where the time goes in v3:
time: 120 us; the launch traced here: 118 us
  Pallas kernels  114 us (95%)
  local copies, waits for them, and re-layouts  3.9 us (3%)
    pallas_call x1, Pallas kernels, body(): pl.pallas_call(kernel, out_shape=jax.ShapeDtypeStruct((4, S, FEAT), bf16)...  114 us

profile of v3, /device:TPU:231, one launch (start us, length us, event | category | flops | bytes accessed | tf_op | source)
XLA Modules:
  0.0 118.1 jit_solution(14506967643779262992)
XLA Ops:
  0.6 1.6 %copy.12.w_ref = bf16[2,20,1280]{2,1,0:T(8,128)(2,1)} copy(bf16[2,20,1280]{2,0,1:T(2,128)(2,1)} %param.13) | data formatting | bytes 204800 | tf_op args[5]
  2.2 113.6 %segment_layer.1 = bf16[4,128,1280]{2,1,0:T(8,128)(2,1)} custom-call(bf16[128,1280]{1,0:T(8,128)(2,1)} %q_ref.1, bf16[128,1280]{1,0:T(8,128)(2,1)} %k_ref.1, bf16[128,1280]{1,0:T(8,128)(2,1)} %v_ref.1, bf16[128,1280]{1,0:T(8,128)(2,1)} %g_ref.1, bf16[128,1280]{1,0:T(8,128)(2,1)} %cache_ref.1, bf16[2,20,1280]{2,1,0:T(8,128)(2,1)} %copy.12.w_ref, ...), custom_call_target="tpu_custom_call" | custom-call | tf_op jit(solution)/shard_map/segment_layer/pallas_call | solution.py:491
  115.8 2.3 %slice_bitcast_fusion = (bf16[128,1280]{1,0:T(8,128)(2,1)}, bf16[128,1280]{1,0:T(8,128)(2,1)}, bf16[128,1280]{1,0:T(8,128)(2,1)}, bf16[128,1280]{1,0:T(8,128)(2,1)}) fusion(bf16[4,128,1280]{2,1,0:T(8,128)(2,1)} %segment_layer.1), kind=kLoop, calls=%fused_computation | loop fusion | bytes 2621440 | tf_op jit(solution)/shard_map/squeeze | solution.py:525

commit v4 on v2

--- a/solution.py
+++ b/solution.py
@@ -15,7 +15,7 @@
 SLOTS = 256
 NEG = -1e30
 KINDS = "XZXXX"
-CHUNKS = ((0, 512), (512, 512), (1024, 256))
+CHUNKS = ((0, 256), (256, 512), (768, 512))
 POOL = 340
 
 

time: 119 us -> 121 us (1.017)
  Pallas kernels: 112 us -> 114 us
    pallas_call x1, Pallas kernels: 112 us -> 114 us  [body(): pl.pallas_call(kernel, out_shape=jax.ShapeDtypeStruct((4, S, FEAT), bf16)...]
where the time goes in v4:
time: 121 us; the launch traced here: 119 us
  Pallas kernels  114 us (94%)
  local copies, waits for them, and re-layouts  3.9 us (3%)
    pallas_call x1, Pallas kernels, body(): pl.pallas_call(kernel, out_shape=jax.ShapeDtypeStruct((4, S, FEAT), bf16)...  114 us

profile of v4, /device:TPU:231, one launch (start us, length us, event | category | flops | bytes accessed | tf_op | source)
XLA Modules:
  0.0 118.7 jit_solution(13972136740921798417)
XLA Ops:
  0.6 1.6 %copy.12.w_ref = bf16[2,20,1280]{2,1,0:T(8,128)(2,1)} copy(bf16[2,20,1280]{2,0,1:T(2,128)(2,1)} %param.13) | data formatting | bytes 204800 | tf_op args[5]
  2.2 114.2 %segment_layer.1 = bf16[4,128,1280]{2,1,0:T(8,128)(2,1)} custom-call(bf16[128,1280]{1,0:T(8,128)(2,1)} %q_ref.1, bf16[128,1280]{1,0:T(8,128)(2,1)} %k_ref.1, bf16[128,1280]{1,0:T(8,128)(2,1)} %v_ref.1, bf16[128,1280]{1,0:T(8,128)(2,1)} %g_ref.1, bf16[128,1280]{1,0:T(8,128)(2,1)} %cache_ref.1, bf16[2,20,1280]{2,1,0:T(8,128)(2,1)} %copy.12.w_ref, ...), custom_call_target="tpu_custom_call" | custom-call | tf_op jit(solution)/shard_map/segment_layer/pallas_call | solution.py:491
  116.4 2.3 %slice_bitcast_fusion = (bf16[128,1280]{1,0:T(8,128)(2,1)}, bf16[128,1280]{1,0:T(8,128)(2,1)}, bf16[128,1280]{1,0:T(8,128)(2,1)}, bf16[128,1280]{1,0:T(8,128)(2,1)}) fusion(bf16[4,128,1280]{2,1,0:T(8,128)(2,1)} %segment_layer.1), kind=kLoop, calls=%fused_computation | loop fusion | bytes 2621440 | tf_op jit(solution)/shard_map/squeeze | solution.py:525
